TPU v7x, 32 devices: a whole 2x2x4 slice. The times are simulated.
32 devices in a mesh: dp: 4 (over z), ctx: 8 (over y, x, core).
Axes of the slice: x: 2, y: 2, z: 4, core: 2. Of those that a mesh axis runs over, the one named last changes fastest.
Arguments:
- queries: bfloat16 [8192, 4096], P(('dp', 'ctx')), parts along dimension 0, may hold values from -5 to 5
- keys_values: bfloat16 [8192, 2, 1024], P(('dp', 'ctx')), parts along dimension 0, may hold values from -5 to 5
- fold: int32 [64], P('dp'), parts along dimension 0, may hold values from 0 to 15, each once
- doc_length: int32 [4], P('dp'), parts along dimension 0, may hold values from 1024 to 2048
Outputs:
- attended: bfloat16 [8192, 4096], P(('dp', 'ctx')), parts along dimension 0
There are 4 independent parts, one for each index of `dp`. A program takes and returns all parts, laid end to end along the dimension named above; each array names one. Nothing has to cross between parts.
Inputs may be any that keep to these rules, and one draw needn't show every extreme that they name: A permutation: slot s, the stored rows s * 128 to (s + 1) * 128 - 1, holds positions fold[s] * 128 onwards. `doc_length`: positions at or beyond it are padding.
All inputs are finite; a program needn't handle non-finite values.
Results may differ from a plain program's by a relative error of at most 0.004.
Values may be sent and summed in bfloat16 or wider, within the bound.
No kernel may reach another device: no remote copies, remote signals or barrier semaphores. Data moves between devices by JAX's collectives and lax.ppermute only.
A program may use at most 320 MiB of HBM per device.

v0:
```python
import functools
import math

import jax
import jax.numpy as jnp
from jax import lax
from jax.experimental import pallas as pl
from jax.experimental.pallas import tpu as pltpu
from jax.sharding import PartitionSpec as P

HEADS = 32
KV_HEADS = 8
HEAD_DIM = 128
GROUP = HEADS // KV_HEADS
LOCAL_HEADS = KV_HEADS // 2
SCALE = math.log2(math.e) / math.sqrt(HEAD_DIM)
LIMIT = 2.0**90
COPY_PIECES = 4
NT = (((1,), (1,)), ((), ()))


class Pack:
    def __init__(self, offset, other):
        self.offset, self.other = offset, other

    def places(self, fold):
        me = lax.axis_index("ctx")
        odd = me % 2
        device = me ^ (self.offset[0] + odd * (self.offset[1] - self.offset[0]) + self.other)
        return [fold[2 * device], fold[2 * device + 1]]


def prepare(kv_hbm, mine_ref, other_ref, kv_ref, sems):
    core = lax.axis_index("ctx") % 2
    half = kv_ref.shape[0] // 2
    rows = kv_ref.shape[0] // COPY_PIECES
    width = mine_ref.shape[4]
    copies = []
    for n in range(COPY_PIECES):
        at = slice(n * rows, (n + 1) * rows)
        copies.append(pltpu.make_async_copy(kv_hbm.at[at], kv_ref.at[at], sems.at[n]))
        copies[-1].start()
    for n in range(COPY_PIECES):
        copies[n].wait()
        j, to = n * rows // half, n * rows % half
        for out_ref, which in ((other_ref, 1 - core), (mine_ref, core)):
            for part in range(2):
                columns = pl.ds(pl.multiple_of((2 * which + part) * width, width), width)
                out_ref[part, j, :, to : to + rows] = jnp.swapaxes(kv_ref[n * rows : (n + 1) * rows, :, columns], 0, 1)


def run_prepare(keys_values):
    rows, two, width = keys_values.shape
    vmem = pl.BlockSpec(memory_space=pltpu.VMEM)
    return pl.pallas_call(
        prepare,
        out_shape=[pltpu.VMEM((2, 2, two, rows // 2, width // 4), jnp.bfloat16)] * 2,
        in_specs=[pl.BlockSpec(memory_space=pl.ANY)],
        out_specs=[vmem, vmem],
        scratch_shapes=[pltpu.VMEM((rows, two, width), jnp.bfloat16), pltpu.SemaphoreType.DMA((COPY_PIECES,))],
        cost_estimate=pl.CostEstimate(flops=1, bytes_accessed=1, transcendentals=0),
        name="prepare",
    )(pltpu.with_memory_space_constraint(keys_values, pltpu.HBM))


def fill_table(fold, length, table):
    for n in range(fold.shape[0]):
        table[n] = fold[n]
    table[fold.shape[0]] = length[0]


def run_fill_table(fold, doc_length):
    smem = pl.BlockSpec(memory_space=pltpu.SMEM)
    return pl.pallas_call(
        fill_table,
        out_shape=pltpu.SMEM((fold.shape[0] + 1,), jnp.int32),
        in_specs=[smem, smem],
        out_specs=smem,
        cost_estimate=pl.CostEstimate(flops=1, bytes_accessed=1, transcendentals=0),
        name="fill_table",
    )(fold, doc_length)


def part_columns(core, part, width):
    return pl.ds(pl.multiple_of((2 * core + part) * width, width), width)


def row_pieces(block, target, columns, sems):
    rows = block.shape[0] // COPY_PIECES
    pieces = [slice(n * rows, (n + 1) * rows) for n in range(COPY_PIECES)]
    return [pltpu.make_async_copy(block.at[at], target.at[at, columns], sems.at[n]) for n, at in enumerate(pieces)]


def place_rest(own, block, attended, out_hbm, sems):
    core = lax.axis_index("ctx") % 2
    copies = []
    for n, (part, which) in enumerate(((own, core), (block, 1 - core))):
        copies += row_pieces(part, out_hbm, part_columns(which, 1, part.shape[1]), sems.at[n])
    for copy in copies:
        copy.start()
    for copy in copies:
        copy.wait()


def run_place_rest(own, block, attended):
    vmem = pl.BlockSpec(memory_space=pltpu.VMEM)
    hbm = pl.BlockSpec(memory_space=pl.ANY)
    return pl.pallas_call(
        place_rest,
        out_shape=jax.ShapeDtypeStruct(attended.shape, attended.dtype),
        in_specs=[vmem, vmem, hbm],
        out_specs=hbm,
        scratch_shapes=[pltpu.SemaphoreType.DMA((2, COPY_PIECES))],
        input_output_aliases={2: 0},
        name="place_rest",
    )(*[pltpu.with_memory_space_constraint(part, pltpu.VMEM) for part in (own, block)], attended)


def stage(held, every_pack, part, sides, continued, *refs):
    refs = list(refs)
    is_first, is_last = part == "first", bool(sides)
    fold = refs[0]
    if is_first:
        q_hbm, q_swapped, *rest = refs[1:]
    else:
        q_ref, *rest = refs[1:]
    packs, rest = rest[: len(held)], rest[len(held) :]
    if not is_first:
        before, rest = rest[0], rest[1:]
    if is_last:
        every, rest = rest[: len(every_pack)], rest[len(every_pack) :]
        if continued:
            arrived, rest = rest[0], rest[2:]
        if 0 in sides:
            out_hbm, rest = rest[0], rest[1:]
        if 1 in sides:
            rest_ref, rest = rest[0], rest[1:]
        if continued:
            out_ref, *rest = rest
            key_buf, value_buf, worst, keys_all, values_all, out_sems, sem = rest
        else:
            key_buf, value_buf, out_ref, worst, keys_all, values_all, out_sems, sem = rest
        if continued:
            columns = part_columns(1 - lax.axis_index("ctx") % 2, 1 - part, arrived.shape[1])
            arrived_copies = row_pieces(arrived, out_hbm, columns, out_sems)
            for copy in arrived_copies:
                copy.start()
        worst[...] = jnp.ones_like(worst)
        heads = range(part * LOCAL_HEADS // 2, (part + 1) * LOCAL_HEADS // 2)
    else:
        heads = range(LOCAL_HEADS)
        if is_first:
            total, q_ref, key_buf, value_buf, q_sems = rest
        else:
            total, key_buf, value_buf = rest
    span_rows = q_ref.shape[0] // 4
    group_rows = GROUP * span_rows
    spans = fold.shape[0]
    me = lax.axis_index("ctx")
    core = me % 2
    length = fold[fold.shape[0] - 1]

    if is_first:
        half, width = q_swapped.shape[0] // 2, q_ref.shape[1]
        columns = pl.ds(pl.multiple_of(core * width, width), width)
        copies = [
            pltpu.make_async_copy(
                source.at[j * half : (j + 1) * half, columns],
                q_ref.at[(2 * n + j) * half : (2 * n + j + 1) * half],
                q_sems.at[2 * n + j],
            )
            for n, source in enumerate((q_hbm, q_swapped))
            for j in range(2)
        ]
        for copy in copies:
            copy.start()

    places = [place for pack in held for place in pack.places(fold)]
    for n, place in enumerate(places):
        rank = sum((other < place).astype(jnp.int32) for other in places)
        at = pl.ds(pl.multiple_of(rank * span_rows, span_rows), span_rows)
        source = packs[n // 2]
        width = source.shape[4]
        wanted = range(source.shape[0]) if not is_last or source.shape[0] == 1 else [part]
        for to, piece in enumerate(wanted):
            key_buf[at, to * width : (to + 1) * width] = source[piece, n % 2, 0]
            value_buf[at, to * width : (to + 1) * width] = source[piece, n % 2, 1]

    def query_place(i):
        return fold[2 * (me ^ (i // 2)) + i % 2]

    def column(head):
        return pl.ds(pl.multiple_of(head * HEAD_DIM, HEAD_DIM), HEAD_DIM)

    def rows_of(i):
        return pl.ds(pl.multiple_of(i * span_rows, span_rows), span_rows)

    def row_in_span():
        return lax.broadcasted_iota(jnp.int32, (group_rows, 1), 0) % span_rows

    def target_of(side):
        return rest_ref if side else out_ref

    def finish(side, i, g, real, sums):
        weight_sum = sums[:, HEAD_DIM:]
        guess = pl.reciprocal(weight_sum, approx=True)
        inverse = guess * (2.0 - weight_sum * guess)
        largest = jnp.maximum(weight_sum, guess).reshape(-1, 8, HEAD_DIM)
        worst[...] = jnp.maximum(worst[...], jnp.where(real, jnp.max(largest, axis=0), 1.0))
        value = (sums[:, :HEAD_DIM] * inverse).astype(jnp.bfloat16)
        for n in range(GROUP):
            target_of(side)[rows_of(i - 2 * side), column((g - heads[0]) * GROUP + n)] = value[
                n * span_rows : (n + 1) * span_rows
            ]

    def product_of(i, g, seen, change):
        query = jnp.concatenate([q_ref[rows_of(i), column(g * GROUP + n)] for n in range(GROUP)], axis=0)
        keys = key_buf[: seen * span_rows, column(g - heads[0])]
        scores = lax.dot_general(query, keys, NT, preferred_element_type=jnp.float32)
        weights = jnp.exp2(scores * SCALE)
        parts = [change(n, weights[:, n * span_rows : (n + 1) * span_rows]) for n in range(seen)]
        weights = jnp.concatenate(parts, axis=1) if seen > 1 else parts[0]
        ones = jnp.ones((seen * span_rows, HEAD_DIM), jnp.bfloat16)
        values = jnp.concatenate([value_buf[: seen * span_rows, column(g - heads[0])], ones], axis=1)
        return jnp.dot(weights.astype(jnp.bfloat16), values, preferred_element_type=jnp.float32)

    def visible_product(i, g):
        place = query_place(i)
        seen = sum((other <= place).astype(jnp.int32) for other in places)

        def change(n, weights):
            if not is_first:
                return jnp.where(seen > n, weights, 0.0)
            col = lax.broadcasted_iota(jnp.int32, (group_rows, span_rows), 1)
            slack = jnp.minimum(row_in_span(), length - 1 - place * span_rows) - col
            least = jnp.where(n == seen - 1, 0, jnp.where(n < seen, -2 * span_rows * spans, 2 * span_rows * spans))
            return jnp.where(slack >= least, weights, 0.0)

        return product_of(i, g, len(places), change)

    def add(i):
        for g in heads:
            total[i, g] = visible_product(i, g) if is_first else total[i, g] + visible_product(i, g)

    def add_last(side):
        for i in (2 * side, 2 * side + 1):
            for g in heads:
                finish(side, i, g, query_place(i) * span_rows < length, before[i, g] + visible_product(i, g))
        ends = [query_place(i) * span_rows + span_rows for i in (2 * side, 2 * side + 1)]

        @pl.when(jnp.maximum(ends[0], ends[1]) > length)
        def _():
            target = target_of(side)
            for i, end in enumerate(ends):
                row = end - span_rows + lax.broadcasted_iota(jnp.int32, (span_rows, target.shape[1]), 0)
                kept = jnp.where(row < length, target[rows_of(i), :].astype(jnp.float32), 0.0)
                target[rows_of(i), :] = kept.astype(jnp.bfloat16)

        if side == 0 and not continued:
            for i in range(2):
                out_copy(i).start()

    def out_copy(i):
        width = out_ref.shape[1]
        columns = part_columns(core, part, width)
        return pltpu.make_async_copy(out_ref.at[rows_of(i)], out_hbm.at[rows_of(i), columns], out_sems.at[i])

    if not is_last:
        for i in range(4):
            if is_first:
                copies[i].wait()
            add(i)
        return
    for side in sides:
        add_last(side)
    if continued:
        for copy in arrived_copies:
            copy.wait()
    elif 0 in sides:
        for i in range(2):
            out_copy(i).wait()

    @pl.when(jnp.logical_not(jnp.max(worst[...]) < LIMIT))
    def _():
        block = 4 * span_rows

        def again(side, step, piece, inside):
            i, n = step // GROUP + 2 * side, step % GROUP
            local = piece * (LOCAL_HEADS // 2) + inside if len(heads) == LOCAL_HEADS else inside
            place = query_place(i)
            query = q_ref[rows_of(i), column((heads[0] + local) * GROUP + n)]
            row = place * span_rows + lax.broadcasted_iota(jnp.int32, (span_rows, 1), 0)

            def masked(k):
                at = pl.ds(pl.multiple_of(k * block, block), block)
                raw = SCALE * lax.dot_general(query, keys_all[at, :], NT, preferred_element_type=jnp.float32)
                key_pos = k * block + lax.broadcasted_iota(jnp.int32, (span_rows, block), 1)
                return raw, key_pos <= jnp.minimum(row, length - 1), at

            def top(k, peak):
                raw, mask, _ = masked(k)
                return jnp.maximum(peak, jnp.max(jnp.where(mask, raw, -1e30), axis=1, keepdims=True))

            blocks = place // 4 + 1
            peak = lax.fori_loop(0, blocks, top, jnp.full((span_rows, 1), -1e30, jnp.float32))

            def more(k, sums):
                raw, mask, at = masked(k)
                weights = jnp.where(mask, jnp.exp2(raw - peak), 0.0)
                product = jnp.dot(weights.astype(jnp.bfloat16), values_all[at, :], preferred_element_type=jnp.float32)
                return sums[0] + product, sums[1] + jnp.sum(weights, axis=1, keepdims=True)

            zero = (jnp.zeros((span_rows, HEAD_DIM), jnp.float32), jnp.zeros((span_rows, 1), jnp.float32))
            numerator, weight_sum = lax.fori_loop(0, blocks, more, zero)
            value = jnp.where(row < length, numerator / weight_sum, 0.0)
            target_of(side)[rows_of(i - 2 * side), column(local * GROUP + n)] = value.astype(jnp.bfloat16)

        def one_head(inside, carry):
            for pack, source in zip(every_pack, every):
                piece = part if source.shape[0] == 2 else 0
                for j, place in enumerate(pack.places(fold)):
                    for kind, target in enumerate((keys_all, values_all)):
                        copy = pltpu.make_async_copy(
                            source.at[piece, j, kind, :, column(inside)], target.at[rows_of(place), :], sem
                        )
                        copy.start()
                        copy.wait()
            for side in sides:

                def one(step, carry):
                    again(side, step, 0, inside)
                    return carry

                lax.fori_loop(0, 2 * GROUP, one, 0)
            return carry

        lax.fori_loop(0, len(heads), one_head, 0)
        if 0 in sides and not continued:
            for i in range(2):
                out_copy(i).start()
                out_copy(i).wait()


def run_stage(table, query_blocks, before, held, everything=(), part=None, sides=(), arrived=None, attended=None):
    is_first, is_last = part == "first", bool(sides)
    span_rows = held[0][1].shape[3]
    width = HEADS // 2 * HEAD_DIM
    vmem = pl.BlockSpec(memory_space=pltpu.VMEM)
    smem = pl.BlockSpec(memory_space=pltpu.SMEM)
    hbm = pl.BlockSpec(memory_space=pl.ANY)
    operands = [table, *query_blocks, *[array for _, array in held]]
    specs = [smem] + [hbm if is_first else vmem] * len(query_blocks) + [vmem] * len(held)
    sums = (4, LOCAL_HEADS, GROUP * span_rows, 2 * HEAD_DIM)
    keys = 2 * len(held) * span_rows
    heads = LOCAL_HEADS // 2 if is_last else LOCAL_HEADS
    scratch = [pltpu.VMEM((keys, heads * HEAD_DIM), jnp.bfloat16)] * 2
    aliases = {}
    if not is_first:
        operands.append(before)
        specs.append(vmem)
    if is_last:
        operands += [array for _, array in everything]
        specs += [hbm] * len(everything)
        if attended is not None:
            operands.append(pltpu.with_memory_space_constraint(arrived, pltpu.VMEM))
            specs.append(vmem)
            aliases = {len(operands): 0}
            operands.append(attended)
            specs.append(hbm)
        out_shape, out_specs = [], []
        if 0 in sides:
            out_shape.append(jax.ShapeDtypeStruct((2 * span_rows, 2 * width), jnp.bfloat16))
            out_specs.append(hbm)
        if 1 in sides or attended is not None:
            out_shape.append(pltpu.VMEM((2 * span_rows, width // 2), jnp.bfloat16))
            out_specs.append(vmem)
        all_keys = 2 * sum(array.shape[0] for _, array in everything if array.shape[0] == 2) // 2 * span_rows
        all_keys += 2 * sum(array.shape[0] == 1 for _, array in everything) * span_rows
        if attended is None:
            scratch = scratch + [pltpu.VMEM((2 * span_rows, width // 2), jnp.bfloat16)]
        scratch = scratch + [
            pltpu.VMEM((8, HEAD_DIM), jnp.float32),
            pltpu.VMEM((all_keys, HEAD_DIM), jnp.bfloat16),
            pltpu.VMEM((all_keys, HEAD_DIM), jnp.bfloat16),
            pltpu.SemaphoreType.DMA((COPY_PIECES,)),
            pltpu.SemaphoreType.DMA,
        ]
    elif is_first:
        out_shape = [pltpu.VMEM(sums, jnp.float32), pltpu.VMEM((4 * span_rows, width), jnp.bfloat16)]
        out_specs = [vmem, vmem]
        scratch = scratch + [pltpu.SemaphoreType.DMA((4,))]
    else:
        out_shape, out_specs = pltpu.VMEM(sums, jnp.float32), vmem
        aliases = {len(operands) - 1: 0}
    return pl.pallas_call(
        functools.partial(
            stage, [pack for pack, _ in held], [pack for pack, _ in everything], part, sides, attended is not None
        ),
        out_shape=out_shape,
        in_specs=specs,
        out_specs=out_specs,
        scratch_shapes=scratch,
        input_output_aliases=aliases,
        compiler_params=pltpu.CompilerParams(vmem_limit_bytes=12 << 20),
        cost_estimate=pl.CostEstimate(flops=1, bytes_accessed=1, transcendentals=0),
        name="stage",
    )(*operands)


def shards(queries, keys_values, fold, doc_length):
    size = lax.axis_size("ctx")

    def swap(name, block, mask=1):
        with jax.named_scope("swap_" + name):
            return lax.ppermute(block, "ctx", [(i, i ^ mask) for i in range(size)])

    def send(name, block, even, odd):
        with jax.named_scope("send_" + name):
            return lax.ppermute(block, "ctx", [(i, i ^ (odd if i % 2 else even)) for i in range(size)])

    query_other = swap("q", queries)
    mine, other = run_prepare(keys_values)
    (fold, doc_length), other = lax.optimization_barrier(((fold, doc_length), other))
    other = swap("kv", other)
    table, other = lax.optimization_barrier((run_fill_table(fold, doc_length), other))
    near, far, across = (2, 4), (4, 2), (6, 6)
    held = [(Pack((0, 0), 0), mine), (Pack((0, 0), 1), other)]
    first = pltpu.with_memory_space_constraint(queries, pltpu.HBM)
    sums, query_block = run_stage(table, (first, query_other), None, held, part="first")

    def after(items, sums):
        arrays, sums = lax.optimization_barrier(([array for _, array in items], sums))
        return [(pack, array) for (pack, _), array in zip(items, arrays)], sums

    def more(items, sums):
        return run_stage(table, (query_block,), sums, items)

    if size == 8:
        a1, b1 = send("a1", mine, 2, 4), send("b1", other, 2, 4)
        (mine, other), sums = lax.optimization_barrier(((mine, other), sums))
        a2, b2 = send("a2", mine, 4, 2), send("b2", other, 4, 2)
        (a1, b1), sums = lax.optimization_barrier(((a1, b1), sums))
        e = send("e", a1, 4, 2)
        f0, f1 = send("f0", b1[:1], 4, 2), send("f1", b1[1:], 4, 2)
        firsts = [(Pack(near, 0), a1), (Pack(near, 1), b1)]
        sums = more(firsts, sums)
        seconds, sums = after([(Pack(far, 0), a2), (Pack(far, 1), b2)], sums)
        sums = more(seconds, sums)
        thirds, sums = after([(Pack(across, 0), e)], sums)
        sums = more(thirds, sums)
        f0, sums = lax.optimization_barrier((f0, sums))
        everything = held + firsts + seconds + thirds
        halves = [f0, f1]
    else:
        got = {0: (mine, other)}
        everything = list(held)
        for offset in range(2, size, 2):
            step = offset & -offset
            got[offset] = [swap("far", block, step) for block in got[offset ^ step]]
            items = [(Pack((offset, offset), n), block) for n, block in enumerate(got[offset])]
            if offset < size - 2:
                sums = more(items, sums)
                everything += items
            else:
                sums = more(items[:1], sums)
                everything += items[:1]
                halves = [items[1][1][:1], items[1][1][1:]]
        across = (size - 2, size - 2)
    last = [(Pack(across, 1), halves[0])]
    attended, rest0 = run_stage(table, (query_block,), sums, last, everything + last, 0, (0, 1))
    rest0 = swap("out0", rest0)
    halves[1], attended = lax.optimization_barrier((halves[1], attended))
    last = [(Pack(across, 1), halves[1])]
    rest1 = run_stage(table, (query_block,), sums, last, everything + last, 1, (1,))[0]
    rest1 = swap("out1", rest1)
    attended, own = run_stage(table, (query_block,), sums, last, everything + last, 1, (0,), rest0, attended)
    return run_place_rest(own, rest1, attended)


def solution(mesh):
    in_specs = (P(("dp", "ctx"), None), P(("dp", "ctx"), None, None), P("dp"), P("dp"))
    out_specs = P(("dp", "ctx"), None)
    return jax.shard_map(shards, mesh=mesh, in_specs=in_specs, out_specs=out_specs, check_vma=False)
```

profile of v0, /device:TPU:22, one launch (start us, length us, event | category | flops | bytes accessed | tf_op | source)
XLA Modules:
  0.0 188.8 jit_solution(17545949546692304819)
XLA Ops:
  0.0 0.0 collective-permute-start.1
  0.0 1.5 prepare.1
  1.5 0.6 collective-permute-start
  2.1 0.5 collective-permute-start.2
  3.3 0.7 fill_table.1.refs_0_
  4.0 1.0 collective-permute-done.refs_4_.refs_5_
  4.9 0.6 collective-permute-start.3
  5.5 0.0 collective-permute-done.1.refs_2_
  5.5 6.6 %stage.7 = (f32[4,4,512,256]{3,2,1,0:T(8,128)S(1)}, bf16[512,2048]{1,0:T(8,128)(2,1)S(1)}) custom-call(s32[17]{0:T(128)S(4)} %fill_table.1.refs_0_, bf16[256,4096]{1,0:T(8,128)(2,1)} %refs_1_.1, bf16[256,4096]{1,0:T(8,128)(2,1)} %collective-permute-done.1.refs_2_, bf16[2,2,2,128,256]{4,3,2,1,0:T(8,128)(2,1)S(1)} %get-tuple-element.45.refs_3_.refs_4_, ...), custom_call_target="tpu_custom_call" | custom-call | flops 1 | bytes 1 | tf_op jit(solution)/shard_map/stage/pallas_call | solution.py:395
  12.1 0.6 collective-permute-start.7
  12.7 1.5 collective-permute-start.8
  14.2 0.0 collective-permute-done.2.refs_2_.refs_6_
  14.2 5.0 %collective-permute-done.3.refs_3_.refs_7_ = bf16[2,2,2,128,256]{4,3,2,1,0:T(8,128)(2,1)S(1)} collective-permute-done((bf16[2,2,2,128,256]{4,3,2,1,0:T(8,128)(2,1)S(1)}, bf16[2,2,2,128,256]{4,3,2,1,0:T(8,128)(2,1)S(1)}, u32[]{:S(2)}, u32[]{:S(2)}) %collective-permute-start.3) | collective-permute-done | bytes 524320 | tf_op jit(solution)/shard_map/send_b1/ppermute | solution.py:419
  19.2 0.0 collective-permute-start.6
  19.2 2.1 %collective-permute-start.5 = (bf16[1,2,2,128,256]{4,3,2,1,0:T(8,128)(2,1)S(1)}, bf16[1,2,2,128,256]{4,3,2,1,0:T(8,128)(2,1)S(1)}, u32[]{:S(2)}, u32[]{:S(2)}) collective-permute-start(bf16[1,2,2,128,256]{4,3,2,1,0:T(8,128)(2,1)S(1)} %get-tuple-element.61), channel_id=1, source_target_pairs={{0,4},{1,3},{2,6},{3,1},{4,0},{5,7},{6,2},{7,5},{8,12},{9,11},{10,... | collective-permute-start | bytes 786440 | tf_op jit(solution)/shard_map/send_f0/ppermute | solution.py:419
  21.3 0.1 collective-permute-start.4
  21.4 4.7 %stage.8.refs_4_ = f32[4,4,512,256]{3,2,1,0:T(8,128)S(1)} custom-call(s32[17]{0:T(128)S(4)} %fill_table.1.refs_0_, bf16[512,2048]{1,0:T(8,128)(2,1)S(1)} %get-tuple-element.40.refs_1_, bf16[2,2,2,128,256]{4,3,2,1,0:T(8,128)(2,1)S(1)} %collective-permute-done.2.refs_2_.refs_6_, ...), custom_call_target="tpu_custom_call", output_to_operand_aliasing={{}: (4, {})} | custom-call | flops 1 | bytes 1 | tf_op jit(solution)/shard_map/stage/pallas_call | solution.py:395
  26.1 0.0 collective-permute-done.7.refs_2_.refs_8_
  26.1 1.1 collective-permute-done.8.refs_3_.refs_9_
  27.2 4.9 %stage.9.refs_3_ = f32[4,4,512,256]{3,2,1,0:T(8,128)S(1)} custom-call(s32[17]{0:T(128)S(4)} %fill_table.1.refs_0_, bf16[512,2048]{1,0:T(8,128)(2,1)S(1)} %get-tuple-element.40.refs_1_, bf16[2,2,2,128,256]{4,3,2,1,0:T(8,128)(2,1)S(1)} %collective-permute-done.7.refs_2_.refs_8_, ...), custom_call_target="tpu_custom_call", output_to_operand_aliasing={{}: (4, {})} | custom-call | flops 1 | bytes 1 | tf_op jit(solution)/shard_map/stage/pallas_call | solution.py:395
  32.1 0.7 collective-permute-done.6.refs_2_.refs_10_
  32.8 2.5 %stage.10.refs_3_ = f32[4,4,512,256]{3,2,1,0:T(8,128)S(1)} custom-call(s32[17]{0:T(128)S(4)} %fill_table.1.refs_0_, bf16[512,2048]{1,0:T(8,128)(2,1)S(1)} %get-tuple-element.40.refs_1_, bf16[2,2,2,128,256]{4,3,2,1,0:T(8,128)(2,1)S(1)} %collective-permute-done.6.refs_2_.refs_10_, f32[4,4,512,256]{3,2,1,0:T(8,128)S(1)} %stage.9.refs_3_), custom_call_target="tpu_custom_call", output_to_operand_aliasing={{}: (3, {})} | custom-call | flops 1 | bytes 1 | tf_op jit(solution)/shard_map/stage/pallas_call | solution.py:395
  35.3 0.3 collective-permute-done.5.refs_2_.refs_11_
  35.7 65.7 %stage.11 = (bf16[256,4096]{1,0:T(8,128)(2,1)}, bf16[256,1024]{1,0:T(8,128)(2,1)S(1)}) custom-call(s32[17]{0:T(128)S(4)} %fill_table.1.refs_0_, bf16[512,2048]{1,0:T(8,128)(2,1)S(1)} %get-tuple-element.40.refs_1_, bf16[1,2,2,128,256]{4,3,2,1,0:T(8,128)(2,1)S(1)} %collective-permute-done.5.refs_2_.refs_11_, f32[4,4,512,256]{3,2,1,0:T(8,128)S(1)} %stage.10.refs_3_, ...), custom_call_target="tpu_custom_call" | custom-call | flops 1 | bytes 1 | tf_op jit(solution)/shard_map/stage/pallas_call | solution.py:395
  101.4 0.0 collective-permute-done.4.refs_2_.refs_11_
  101.4 1.1 collective-permute-start.9
  102.5 22.3 %stage.13 = bf16[256,1024]{1,0:T(8,128)(2,1)S(1)} custom-call(s32[17]{0:T(128)S(4)} %fill_table.1.refs_0_, bf16[512,2048]{1,0:T(8,128)(2,1)S(1)} %get-tuple-element.40.refs_1_, bf16[1,2,2,128,256]{4,3,2,1,0:T(8,128)(2,1)S(1)} %collective-permute-done.4.refs_2_.refs_11_, f32[4,4,512,256]{3,2,1,0:T(8,128)S(1)} %stage.10.refs_3_, ...), custom_call_target="tpu_custom_call" | custom-call | flops 1 | bytes 1 | tf_op jit(solution)/shard_map/stage/pallas_call | solution.py:395
  124.8 20.0 %collective-permute-start.10 = (bf16[256,1024]{1,0:T(8,128)(2,1)S(1)}, bf16[256,1024]{1,0:T(8,128)(2,1)S(1)}, u32[]{:S(2)}, u32[]{:S(2)}) collective-permute-start(bf16[256,1024]{1,0:T(8,128)(2,1)S(1)} %stage.13), channel_id=1, source_target_pairs={{0,1},{1,0},{2,3},{3,2},{4,5},{5,4},{6,7},{7,6},{8,9},{9,8},{10,11... | collective-permute-start | bytes 1572872 | tf_op jit(solution)/shard_map/swap_out1/ppermute | solution.py:415
  144.8 0.0 collective-permute-done.9.refs_12_
  144.8 42.8 %stage.12 = (bf16[256,4096]{1,0:T(8,128)(2,1)}, bf16[256,1024]{1,0:T(8,128)(2,1)S(1)}) custom-call(s32[17]{0:T(128)S(4)} %fill_table.1.refs_0_, bf16[512,2048]{1,0:T(8,128)(2,1)S(1)} %get-tuple-element.40.refs_1_, bf16[1,2,2,128,256]{4,3,2,1,0:T(8,128)(2,1)S(1)} %collective-permute-done.4.refs_2_.refs_11_, ...), custom_call_target="tpu_custom_call", output_to_operand_aliasing={{0}: (13, {})} | custom-call | flops 1 | bytes 1 | tf_op jit(solution)/shard_map/stage/pallas_call | solution.py:395
  187.6 0.0 collective-permute-done.10.block
  187.6 1.0 place_rest.1
  (1 shorter events, 0.0 us)
Async XLA Ops:
  0.0 5.5 %collective-permute-start.1 = (bf16[256,4096]{1,0:T(8,128)(2,1)}, bf16[256,4096]{1,0:T(8,128)(2,1)}, u32[]{:S(2)}, u32[]{:S(2)}) collective-permute-start(bf16[256,4096]{1,0:T(8,128)(2,1)} %refs_1_.1), channel_id=1, source_target_pairs={{0,1},{1,0},{2,3},{3,2},{4,5},{5,4},{6,7},{7,6},{8,9},{9,8},{10,11... | collective-permute-start | bytes 6291464 | tf_op jit(solution)/shard_map/swap_q/ppermute | solution.py:415
  1.5 3.4 %collective-permute-start = (bf16[2,2,2,128,256]{4,3,2,1,0:T(8,128)(2,1)S(1)}, bf16[2,2,2,128,256]{4,3,2,1,0:T(8,128)(2,1)S(1)}, u32[]{:S(2)}, u32[]{:S(2)}) collective-permute-start(bf16[2,2,2,128,256]{4,3,2,1,0:T(8,128)(2,1)S(1)} %get-tuple-element.36), channel_id=1, source_target_pairs={{0,1},{1,0},{2,3},{3,2},{4,5},{5,4},{6,7},{7,6},{8,9},{9,8},{10,11... | collective-permute-start | bytes 1572872 | tf_op jit(solution)/shard_map/swap_kv/ppermute | solution.py:415
  2.1 12.1 %collective-permute-start.2 = (bf16[2,2,2,128,256]{4,3,2,1,0:T(8,128)(2,1)S(1)}, bf16[2,2,2,128,256]{4,3,2,1,0:T(8,128)(2,1)S(1)}, u32[]{:S(2)}, u32[]{:S(2)}) collective-permute-start(bf16[2,2,2,128,256]{4,3,2,1,0:T(8,128)(2,1)S(1)} %get-tuple-element.45.refs_3_.refs_4_), channel_id=1, source_target_pairs={{0,2},{1,5},{2,0},{3,7},{4,6},{5,1},{6,4},{7,3},{8,10},{9,13},{10,... | collective-permute-start | bytes 1572872 | tf_op jit(solution)/shard_map/send_a1/ppermute | solution.py:419
  4.9 14.3 %collective-permute-start.3 = (bf16[2,2,2,128,256]{4,3,2,1,0:T(8,128)(2,1)S(1)}, bf16[2,2,2,128,256]{4,3,2,1,0:T(8,128)(2,1)S(1)}, u32[]{:S(2)}, u32[]{:S(2)}) collective-permute-start(bf16[2,2,2,128,256]{4,3,2,1,0:T(8,128)(2,1)S(1)} %collective-permute-done.refs_4_.refs_5_), channel_id=1, source_target_pairs={{0,2},{1,5},{2,0},{3,7},{4,6},{5,1},{6,4},{7,3},{8,10},{9,13},{10,... | collective-permute-start | bytes 1572872 | tf_op jit(solution)/shard_map/send_b1/ppermute | solution.py:419
  12.1 14.0 %collective-permute-start.7 = (bf16[2,2,2,128,256]{4,3,2,1,0:T(8,128)(2,1)S(1)}, bf16[2,2,2,128,256]{4,3,2,1,0:T(8,128)(2,1)S(1)}, u32[]{:S(2)}, u32[]{:S(2)}) collective-permute-start(bf16[2,2,2,128,256]{4,3,2,1,0:T(8,128)(2,1)S(1)} %get-tuple-element.45.refs_3_.refs_4_), channel_id=1, source_target_pairs={{0,4},{1,3},{2,6},{3,1},{4,0},{5,7},{6,2},{7,5},{8,12},{9,11},{10,... | collective-permute-start | bytes 1572872 | tf_op jit(solution)/shard_map/send_a2/ppermute | solution.py:419
  12.7 14.6 %collective-permute-start.8 = (bf16[2,2,2,128,256]{4,3,2,1,0:T(8,128)(2,1)S(1)}, bf16[2,2,2,128,256]{4,3,2,1,0:T(8,128)(2,1)S(1)}, u32[]{:S(2)}, u32[]{:S(2)}) collective-permute-start(bf16[2,2,2,128,256]{4,3,2,1,0:T(8,128)(2,1)S(1)} %collective-permute-done.refs_4_.refs_5_), channel_id=1, source_target_pairs={{0,4},{1,3},{2,6},{3,1},{4,0},{5,7},{6,2},{7,5},{8,12},{9,11},{10,... | collective-permute-start | bytes 1572872 | tf_op jit(solution)/shard_map/send_b2/ppermute | solution.py:419
  19.2 13.7 %collective-permute-start.6 = (bf16[2,2,2,128,256]{4,3,2,1,0:T(8,128)(2,1)S(1)}, bf16[2,2,2,128,256]{4,3,2,1,0:T(8,128)(2,1)S(1)}, u32[]{:S(2)}, u32[]{:S(2)}) collective-permute-start(bf16[2,2,2,128,256]{4,3,2,1,0:T(8,128)(2,1)S(1)} %collective-permute-done.2.refs_2_.refs_6_), channel_id=1, source_target_pairs={{0,4},{1,3},{2,6},{3,1},{4,0},{5,7},{6,2},{7,5},{8,12},{9,11},{10,... | collective-permute-start | bytes 1572872 | tf_op jit(solution)/shard_map/send_e/ppermute | solution.py:419
  19.2 16.4 %collective-permute-start.5 = (bf16[1,2,2,128,256]{4,3,2,1,0:T(8,128)(2,1)S(1)}, bf16[1,2,2,128,256]{4,3,2,1,0:T(8,128)(2,1)S(1)}, u32[]{:S(2)}, u32[]{:S(2)}) collective-permute-start(bf16[1,2,2,128,256]{4,3,2,1,0:T(8,128)(2,1)S(1)} %get-tuple-element.61), channel_id=1, source_target_pairs={{0,4},{1,3},{2,6},{3,1},{4,0},{5,7},{6,2},{7,5},{8,12},{9,11},{10,... | collective-permute-start | bytes 786440 | tf_op jit(solution)/shard_map/send_f0/ppermute | solution.py:419
  21.3 80.1 %collective-permute-start.4 = (bf16[1,2,2,128,256]{4,3,2,1,0:T(8,128)(2,1)S(1)}, bf16[1,2,2,128,256]{4,3,2,1,0:T(8,128)(2,1)S(1)}, u32[]{:S(2)}, u32[]{:S(2)}) collective-permute-start(bf16[1,2,2,128,256]{4,3,2,1,0:T(8,128)(2,1)S(1)} %get-tuple-element.62), channel_id=1, source_target_pairs={{0,4},{1,3},{2,6},{3,1},{4,0},{5,7},{6,2},{7,5},{8,12},{9,11},{10,... | collective-permute-start | bytes 786440 | tf_op jit(solution)/shard_map/send_f1/ppermute | solution.py:419
  101.4 43.4 %collective-permute-start.9 = (bf16[256,1024]{1,0:T(8,128)(2,1)S(1)}, bf16[256,1024]{1,0:T(8,128)(2,1)S(1)}, u32[]{:S(2)}, u32[]{:S(2)}) collective-permute-start(bf16[256,1024]{1,0:T(8,128)(2,1)S(1)} %get-tuple-element.57), channel_id=1, source_target_pairs={{0,1},{1,0},{2,3},{3,2},{4,5},{5,4},{6,7},{7,6},{8,9},{9,8},{10,11... | collective-permute-start | bytes 1572872 | tf_op jit(solution)/shard_map/swap_out0/ppermute | solution.py:415
  124.8 62.8 %collective-permute-start.10 = (bf16[256,1024]{1,0:T(8,128)(2,1)S(1)}, bf16[256,1024]{1,0:T(8,128)(2,1)S(1)}, u32[]{:S(2)}, u32[]{:S(2)}) collective-permute-start(bf16[256,1024]{1,0:T(8,128)(2,1)S(1)} %stage.13), channel_id=1, source_target_pairs={{0,1},{1,0},{2,3},{3,2},{4,5},{5,4},{6,7},{7,6},{8,9},{9,8},{10,11... | collective-permute-start | bytes 1572872 | tf_op jit(solution)/shard_map/swap_out1/ppermute | solution.py:415
where the time goes:
time: 192 us; the launch traced here: 189 us
  Pallas kernels  153 us (80%)
  starting transfers between devices  27.1 us (14%)
  waiting for transfers between devices  8.12 us (4%)
    pallas_call x7, Pallas kernels, run_stage(): pl.pallas_call(functools.partial(stage, [pack for pack, _ in held], [pack...  150 us
    ppermute x4, starting transfers between devices, swap(): return lax.ppermute(block, 'ctx', [(i, i ^ mask) for i in range(size)])  21.6 us
    ppermute x7, waiting for transfers between devices, send(): lax.ppermute(block, 'ctx', [(i, i ^ (odd if i % 2 else even)) for i in ra...  7.15 us
    ppermute x7, starting transfers between devices, send(): lax.ppermute(block, 'ctx', [(i, i ^ (odd if i % 2 else even)) for i in ra...  5.41 us
  transfers between devices with their start and end apart: 11, of which 5 were waited for; matrix products, arithmetic and copies ran while one was open for 0% of the time, Pallas kernels for 80%

commit v1 on v0

--- a/solution.py
+++ b/solution.py
@@ -85,35 +85,32 @@
     return pl.ds(pl.multiple_of((2 * core + part) * width, width), width)
 
 
-def row_pieces(block, target, columns, sems):
-    rows = block.shape[0] // COPY_PIECES
-    pieces = [slice(n * rows, (n + 1) * rows) for n in range(COPY_PIECES)]
-    return [pltpu.make_async_copy(block.at[at], target.at[at, columns], sems.at[n]) for n, at in enumerate(pieces)]
-
-
-def place_rest(own, block, attended, out_hbm, sems):
+def place_rest(own, block0, block1, attended, out_hbm, sems):
     core = lax.axis_index("ctx") % 2
-    copies = []
-    for n, (part, which) in enumerate(((own, core), (block, 1 - core))):
-        copies += row_pieces(part, out_hbm, part_columns(which, 1, part.shape[1]), sems.at[n])
+    pieces = ((own, core, 1), (block1, 1 - core, 1), (block0, 1 - core, 0))
+    copies = [
+        pltpu.make_async_copy(piece, out_hbm.at[:, part_columns(which, part, piece.shape[1])], sems.at[n])
+        for n, (piece, which, part) in enumerate(pieces)
+    ]
     for copy in copies:
         copy.start()
     for copy in copies:
         copy.wait()
 
 
-def run_place_rest(own, block, attended):
+def run_place_rest(own, block0, block1, attended):
     vmem = pl.BlockSpec(memory_space=pltpu.VMEM)
     hbm = pl.BlockSpec(memory_space=pl.ANY)
     return pl.pallas_call(
         place_rest,
         out_shape=jax.ShapeDtypeStruct(attended.shape, attended.dtype),
-        in_specs=[vmem, vmem, hbm],
+        in_specs=[vmem, vmem, vmem, hbm],
         out_specs=hbm,
-        scratch_shapes=[pltpu.SemaphoreType.DMA((2, COPY_PIECES))],
-        input_output_aliases={2: 0},
+        scratch_shapes=[pltpu.SemaphoreType.DMA((3,))],
+        input_output_aliases={3: 0},
+        compiler_params=pltpu.CompilerParams(vmem_limit_bytes=4 << 20),
         name="place_rest",
-    )(*[pltpu.with_memory_space_constraint(part, pltpu.VMEM) for part in (own, block)], attended)
+    )(*[pltpu.with_memory_space_constraint(part, pltpu.VMEM) for part in (own, block0, block1)], attended)
 
 
 def stage(held, every_pack, part, sides, continued, *refs):
@@ -129,9 +126,7 @@
         before, rest = rest[0], rest[1:]
     if is_last:
         every, rest = rest[: len(every_pack)], rest[len(every_pack) :]
-        if continued:
-            arrived, rest = rest[0], rest[2:]
-        if 0 in sides:
+        if 0 in sides and not continued:
             out_hbm, rest = rest[0], rest[1:]
         if 1 in sides:
             rest_ref, rest = rest[0], rest[1:]
@@ -140,11 +135,6 @@
             key_buf, value_buf, worst, keys_all, values_all, out_sems, sem = rest
         else:
             key_buf, value_buf, out_ref, worst, keys_all, values_all, out_sems, sem = rest
-        if continued:
-            columns = part_columns(1 - lax.axis_index("ctx") % 2, 1 - part, arrived.shape[1])
-            arrived_copies = row_pieces(arrived, out_hbm, columns, out_sems)
-            for copy in arrived_copies:
-                copy.start()
         worst[...] = jnp.ones_like(worst)
         heads = range(part * LOCAL_HEADS // 2, (part + 1) * LOCAL_HEADS // 2)
     else:
@@ -273,10 +263,7 @@
         return
     for side in sides:
         add_last(side)
-    if continued:
-        for copy in arrived_copies:
-            copy.wait()
-    elif 0 in sides:
+    if 0 in sides and not continued:
         for i in range(2):
             out_copy(i).wait()
 
@@ -341,7 +328,7 @@
                 out_copy(i).wait()
 
 
-def run_stage(table, query_blocks, before, held, everything=(), part=None, sides=(), arrived=None, attended=None):
+def run_stage(table, query_blocks, before, held, everything=(), part=None, sides=(), continued=False):
     is_first, is_last = part == "first", bool(sides)
     span_rows = held[0][1].shape[3]
     width = HEADS // 2 * HEAD_DIM
@@ -361,22 +348,16 @@
     if is_last:
         operands += [array for _, array in everything]
         specs += [hbm] * len(everything)
-        if attended is not None:
-            operands.append(pltpu.with_memory_space_constraint(arrived, pltpu.VMEM))
-            specs.append(vmem)
-            aliases = {len(operands): 0}
-            operands.append(attended)
-            specs.append(hbm)
         out_shape, out_specs = [], []
-        if 0 in sides:
+        if 0 in sides and not continued:
             out_shape.append(jax.ShapeDtypeStruct((2 * span_rows, 2 * width), jnp.bfloat16))
             out_specs.append(hbm)
-        if 1 in sides or attended is not None:
+        if 1 in sides or continued:
             out_shape.append(pltpu.VMEM((2 * span_rows, width // 2), jnp.bfloat16))
             out_specs.append(vmem)
         all_keys = 2 * sum(array.shape[0] for _, array in everything if array.shape[0] == 2) // 2 * span_rows
         all_keys += 2 * sum(array.shape[0] == 1 for _, array in everything) * span_rows
-        if attended is None:
+        if not continued:
             scratch = scratch + [pltpu.VMEM((2 * span_rows, width // 2), jnp.bfloat16)]
         scratch = scratch + [
             pltpu.VMEM((8, HEAD_DIM), jnp.float32),
@@ -394,7 +375,7 @@
         aliases = {len(operands) - 1: 0}
     return pl.pallas_call(
         functools.partial(
-            stage, [pack for pack, _ in held], [pack for pack, _ in everything], part, sides, attended is not None
+            stage, [pack for pack, _ in held], [pack for pack, _ in everything], part, sides, continued
         ),
         out_shape=out_shape,
         in_specs=specs,
@@ -473,8 +454,10 @@
     last = [(Pack(across, 1), halves[1])]
     rest1 = run_stage(table, (query_block,), sums, last, everything + last, 1, (1,))[0]
     rest1 = swap("out1", rest1)
-    attended, own = run_stage(table, (query_block,), sums, last, everything + last, 1, (0,), rest0, attended)
-    return run_place_rest(own, rest1, attended)
+    (rest0, block), sums = lax.optimization_barrier(((rest0, halves[1]), sums))
+    last = [(Pack(across, 1), block)]
+    own = run_stage(table, (query_block,), sums, last, everything + last, 1, (0,), True)[0]
+    return run_place_rest(own, rest0, rest1, attended)
 
 
 def solution(mesh):

time: 192 us -> 182 us (0.948)
  the two profiles are of different devices: /device:TPU:22 before, /device:TPU:13 now
where the time goes in v1:
time: 182 us; the launch traced here: 179 us
  Pallas kernels  153 us (84%)
  starting transfers between devices  16.3 us (9%)
  waiting for transfers between devices  9.53 us (5%)
    pallas_call x7, Pallas kernels, run_stage(): pl.pallas_call(functools.partial(stage, [pack for pack, _ in held], [pack...  149 us
    ppermute x4, starting transfers between devices, swap(): return lax.ppermute(block, 'ctx', [(i, i ^ mask) for i in range(size)])  11.3 us
    ppermute x7, waiting for transfers between devices, send(): lax.ppermute(block, 'ctx', [(i, i ^ (odd if i % 2 else even)) for i in ra...  8.2 us
    ppermute x7, starting transfers between devices, send(): lax.ppermute(block, 'ctx', [(i, i ^ (odd if i % 2 else even)) for i in ra...  4.99 us
  transfers between devices with their start and end apart: 11, of which 5 were waited for; matrix products, arithmetic and copies ran while one was open for 0% of the time, Pallas kernels for 84%

profile of v1, /device:TPU:13, one launch (start us, length us, event | category | flops | bytes accessed | tf_op | source)
XLA Modules:
  0.0 179.3 jit_solution(14639871263953004026)
XLA Ops:
  0.0 0.7 collective-permute-start.1
  0.7 1.5 prepare.1
  2.2 0.1 collective-permute-start
  2.3 0.3 collective-permute-start.2
  3.2 0.7 fill_table.1.refs_0_
  3.9 1.3 collective-permute-done.refs_4_.refs_5_
  5.2 0.2 collective-permute-start.3
  5.4 0.0 collective-permute-done.1.refs_2_
  5.4 6.6 %stage.7 = (f32[4,4,512,256]{3,2,1,0:T(8,128)S(1)}, bf16[512,2048]{1,0:T(8,128)(2,1)S(1)}) custom-call(s32[17]{0:T(128)S(4)} %fill_table.1.refs_0_, bf16[256,4096]{1,0:T(8,128)(2,1)} %refs_1_.1, bf16[256,4096]{1,0:T(8,128)(2,1)} %collective-permute-done.1.refs_2_, bf16[2,2,2,128,256]{4,3,2,1,0:T(8,128)(2,1)S(1)} %get-tuple-element.46.refs_3_.refs_4_, ...), custom_call_target="tpu_custom_call" | custom-call | flops 1 | bytes 1 | tf_op jit(solution)/shard_map/stage/pallas_call | solution.py:376
  12.0 1.3 collective-permute-start.6
  13.3 0.3 collective-permute-start.7
  13.5 0.0 collective-permute-done.2.refs_2_.refs_6_
  13.5 2.7 %collective-permute-done.3.refs_3_.refs_7_ = bf16[2,2,2,128,256]{4,3,2,1,0:T(8,128)(2,1)S(1)} collective-permute-done((bf16[2,2,2,128,256]{4,3,2,1,0:T(8,128)(2,1)S(1)}, bf16[2,2,2,128,256]{4,3,2,1,0:T(8,128)(2,1)S(1)}, u32[]{:S(2)}, u32[]{:S(2)}) %collective-permute-start.3) | collective-permute-done | bytes 524320 | tf_op jit(solution)/shard_map/send_b1/ppermute | solution.py:400
  16.3 1.4 collective-permute-start.5
  17.7 0.1 collective-permute-start.4
  17.8 1.4 collective-permute-start.9
  19.3 4.7 %stage.8.refs_4_ = f32[4,4,512,256]{3,2,1,0:T(8,128)S(1)} custom-call(s32[17]{0:T(128)S(4)} %fill_table.1.refs_0_, bf16[512,2048]{1,0:T(8,128)(2,1)S(1)} %get-tuple-element.41.refs_1_, bf16[2,2,2,128,256]{4,3,2,1,0:T(8,128)(2,1)S(1)} %collective-permute-done.2.refs_2_.refs_6_, ...), custom_call_target="tpu_custom_call", output_to_operand_aliasing={{}: (4, {})} | custom-call | flops 1 | bytes 1 | tf_op jit(solution)/shard_map/stage/pallas_call | solution.py:376
  24.0 0.0 collective-permute-done.6.refs_2_.refs_8_
  24.0 4.4 %collective-permute-done.7.refs_3_.refs_9_ = bf16[2,2,2,128,256]{4,3,2,1,0:T(8,128)(2,1)S(1)} collective-permute-done((bf16[2,2,2,128,256]{4,3,2,1,0:T(8,128)(2,1)S(1)}, bf16[2,2,2,128,256]{4,3,2,1,0:T(8,128)(2,1)S(1)}, u32[]{:S(2)}, u32[]{:S(2)}) %collective-permute-start.7) | collective-permute-done | bytes 524320 | tf_op jit(solution)/shard_map/send_b2/ppermute | solution.py:400
  28.4 4.9 %stage.9.refs_3_ = f32[4,4,512,256]{3,2,1,0:T(8,128)S(1)} custom-call(s32[17]{0:T(128)S(4)} %fill_table.1.refs_0_, bf16[512,2048]{1,0:T(8,128)(2,1)S(1)} %get-tuple-element.41.refs_1_, bf16[2,2,2,128,256]{4,3,2,1,0:T(8,128)(2,1)S(1)} %collective-permute-done.6.refs_2_.refs_8_, ...), custom_call_target="tpu_custom_call", output_to_operand_aliasing={{}: (4, {})} | custom-call | flops 1 | bytes 1 | tf_op jit(solution)/shard_map/stage/pallas_call | solution.py:376
  33.3 0.7 collective-permute-done.5.refs_2_.refs_10_
  34.0 2.5 %stage.10.refs_3_ = f32[4,4,512,256]{3,2,1,0:T(8,128)S(1)} custom-call(s32[17]{0:T(128)S(4)} %fill_table.1.refs_0_, bf16[512,2048]{1,0:T(8,128)(2,1)S(1)} %get-tuple-element.41.refs_1_, bf16[2,2,2,128,256]{4,3,2,1,0:T(8,128)(2,1)S(1)} %collective-permute-done.5.refs_2_.refs_10_, f32[4,4,512,256]{3,2,1,0:T(8,128)S(1)} %stage.9.refs_3_), custom_call_target="tpu_custom_call", output_to_operand_aliasing={{}: (3, {})} | custom-call | flops 1 | bytes 1 | tf_op jit(solution)/shard_map/stage/pallas_call | solution.py:376
  36.5 0.3 collective-permute-done.4.refs_2_.refs_11_
  36.8 65.8 %stage.11 = (bf16[256,4096]{1,0:T(8,128)(2,1)}, bf16[256,1024]{1,0:T(8,128)(2,1)S(1)}) custom-call(s32[17]{0:T(128)S(4)} %fill_table.1.refs_0_, bf16[512,2048]{1,0:T(8,128)(2,1)S(1)} %get-tuple-element.41.refs_1_, bf16[1,2,2,128,256]{4,3,2,1,0:T(8,128)(2,1)S(1)} %collective-permute-done.4.refs_2_.refs_11_, f32[4,4,512,256]{3,2,1,0:T(8,128)S(1)} %stage.10.refs_3_, ...), custom_call_target="tpu_custom_call" | custom-call | flops 1 | bytes 1 | tf_op jit(solution)/shard_map/stage/pallas_call | solution.py:376
  102.6 0.2 collective-permute-start.8
  102.8 0.0 collective-permute-done.9.refs_2_.refs_11_
  102.8 27.4 %stage.13 = bf16[256,1024]{1,0:T(8,128)(2,1)S(1)} custom-call(s32[17]{0:T(128)S(4)} %fill_table.1.refs_0_, bf16[512,2048]{1,0:T(8,128)(2,1)S(1)} %get-tuple-element.41.refs_1_, bf16[1,2,2,128,256]{4,3,2,1,0:T(8,128)(2,1)S(1)} %collective-permute-done.9.refs_2_.refs_11_, f32[4,4,512,256]{3,2,1,0:T(8,128)S(1)} %stage.10.refs_3_, ...), custom_call_target="tpu_custom_call" | custom-call | flops 1 | bytes 1 | tf_op jit(solution)/shard_map/stage/pallas_call | solution.py:376
  130.2 10.4 %collective-permute-start.10 = (bf16[256,1024]{1,0:T(8,128)(2,1)S(1)}, bf16[256,1024]{1,0:T(8,128)(2,1)S(1)}, u32[]{:S(2)}, u32[]{:S(2)}) collective-permute-start(bf16[256,1024]{1,0:T(8,128)(2,1)S(1)} %stage.13), channel_id=1, source_target_pairs={{0,1},{1,0},{2,3},{3,2},{4,5},{5,4},{6,7},{7,6},{8,9},{9,8},{10,11... | collective-permute-start | bytes 1572872 | tf_op jit(solution)/shard_map/swap_out1/ppermute | solution.py:396
  140.6 0.0 collective-permute-done.8.block0
  140.6 37.3 %stage.12.own = bf16[256,1024]{1,0:T(8,128)(2,1)S(1)} custom-call(s32[17]{0:T(128)S(4)} %fill_table.1.refs_0_, bf16[512,2048]{1,0:T(8,128)(2,1)S(1)} %get-tuple-element.41.refs_1_, bf16[1,2,2,128,256]{4,3,2,1,0:T(8,128)(2,1)S(1)} %collective-permute-done.9.refs_2_.refs_11_, f32[4,4,512,256]{3,2,1,0:T(8,128)S(1)} %stage.10.refs_3_, ...), custom_call_target="tpu_custom_call" | custom-call | flops 1 | bytes 1 | tf_op jit(solution)/shard_map/stage/pallas_call | solution.py:376
  178.0 0.0 collective-permute-done.10.block1
  178.0 1.2 place_rest.1
  (1 shorter events, 0.0 us)
Async XLA Ops:
  0.0 5.4 %collective-permute-start.1 = (bf16[256,4096]{1,0:T(8,128)(2,1)}, bf16[256,4096]{1,0:T(8,128)(2,1)}, u32[]{:S(2)}, u32[]{:S(2)}) collective-permute-start(bf16[256,4096]{1,0:T(8,128)(2,1)} %refs_1_.1), channel_id=1, source_target_pairs={{0,1},{1,0},{2,3},{3,2},{4,5},{5,4},{6,7},{7,6},{8,9},{9,8},{10,11... | collective-permute-start | bytes 6291464 | tf_op jit(solution)/shard_map/swap_q/ppermute | solution.py:396
  2.2 3.0 %collective-permute-start = (bf16[2,2,2,128,256]{4,3,2,1,0:T(8,128)(2,1)S(1)}, bf16[2,2,2,128,256]{4,3,2,1,0:T(8,128)(2,1)S(1)}, u32[]{:S(2)}, u32[]{:S(2)}) collective-permute-start(bf16[2,2,2,128,256]{4,3,2,1,0:T(8,128)(2,1)S(1)} %get-tuple-element.37), channel_id=1, source_target_pairs={{0,1},{1,0},{2,3},{3,2},{4,5},{5,4},{6,7},{7,6},{8,9},{9,8},{10,11... | collective-permute-start | bytes 1572872 | tf_op jit(solution)/shard_map/swap_kv/ppermute | solution.py:396
  2.3 11.3 %collective-permute-start.2 = (bf16[2,2,2,128,256]{4,3,2,1,0:T(8,128)(2,1)S(1)}, bf16[2,2,2,128,256]{4,3,2,1,0:T(8,128)(2,1)S(1)}, u32[]{:S(2)}, u32[]{:S(2)}) collective-permute-start(bf16[2,2,2,128,256]{4,3,2,1,0:T(8,128)(2,1)S(1)} %get-tuple-element.46.refs_3_.refs_4_), channel_id=1, source_target_pairs={{0,2},{1,5},{2,0},{3,7},{4,6},{5,1},{6,4},{7,3},{8,10},{9,13},{10,... | collective-permute-start | bytes 1572872 | tf_op jit(solution)/shard_map/send_a1/ppermute | solution.py:400
  5.2 11.1 %collective-permute-start.3 = (bf16[2,2,2,128,256]{4,3,2,1,0:T(8,128)(2,1)S(1)}, bf16[2,2,2,128,256]{4,3,2,1,0:T(8,128)(2,1)S(1)}, u32[]{:S(2)}, u32[]{:S(2)}) collective-permute-start(bf16[2,2,2,128,256]{4,3,2,1,0:T(8,128)(2,1)S(1)} %collective-permute-done.refs_4_.refs_5_), channel_id=1, source_target_pairs={{0,2},{1,5},{2,0},{3,7},{4,6},{5,1},{6,4},{7,3},{8,10},{9,13},{10,... | collective-permute-start | bytes 1572872 | tf_op jit(solution)/shard_map/send_b1/ppermute | solution.py:400
  12.0 11.9 %collective-permute-start.6 = (bf16[2,2,2,128,256]{4,3,2,1,0:T(8,128)(2,1)S(1)}, bf16[2,2,2,128,256]{4,3,2,1,0:T(8,128)(2,1)S(1)}, u32[]{:S(2)}, u32[]{:S(2)}) collective-permute-start(bf16[2,2,2,128,256]{4,3,2,1,0:T(8,128)(2,1)S(1)} %get-tuple-element.46.refs_3_.refs_4_), channel_id=1, source_target_pairs={{0,4},{1,3},{2,6},{3,1},{4,0},{5,7},{6,2},{7,5},{8,12},{9,11},{10,... | collective-permute-start | bytes 1572872 | tf_op jit(solution)/shard_map/send_a2/ppermute | solution.py:400
  13.3 15.1 %collective-permute-start.7 = (bf16[2,2,2,128,256]{4,3,2,1,0:T(8,128)(2,1)S(1)}, bf16[2,2,2,128,256]{4,3,2,1,0:T(8,128)(2,1)S(1)}, u32[]{:S(2)}, u32[]{:S(2)}) collective-permute-start(bf16[2,2,2,128,256]{4,3,2,1,0:T(8,128)(2,1)S(1)} %collective-permute-done.refs_4_.refs_5_), channel_id=1, source_target_pairs={{0,4},{1,3},{2,6},{3,1},{4,0},{5,7},{6,2},{7,5},{8,12},{9,11},{10,... | collective-permute-start | bytes 1572872 | tf_op jit(solution)/shard_map/send_b2/ppermute | solution.py:400
  16.3 17.7 %collective-permute-start.5 = (bf16[2,2,2,128,256]{4,3,2,1,0:T(8,128)(2,1)S(1)}, bf16[2,2,2,128,256]{4,3,2,1,0:T(8,128)(2,1)S(1)}, u32[]{:S(2)}, u32[]{:S(2)}) collective-permute-start(bf16[2,2,2,128,256]{4,3,2,1,0:T(8,128)(2,1)S(1)} %collective-permute-done.2.refs_2_.refs_6_), channel_id=1, source_target_pairs={{0,4},{1,3},{2,6},{3,1},{4,0},{5,7},{6,2},{7,5},{8,12},{9,11},{10,... | collective-permute-start | bytes 1572872 | tf_op jit(solution)/shard_map/send_e/ppermute | solution.py:400
  17.7 19.1 %collective-permute-start.4 = (bf16[1,2,2,128,256]{4,3,2,1,0:T(8,128)(2,1)S(1)}, bf16[1,2,2,128,256]{4,3,2,1,0:T(8,128)(2,1)S(1)}, u32[]{:S(2)}, u32[]{:S(2)}) collective-permute-start(bf16[1,2,2,128,256]{4,3,2,1,0:T(8,128)(2,1)S(1)} %get-tuple-element.64), channel_id=1, source_target_pairs={{0,4},{1,3},{2,6},{3,1},{4,0},{5,7},{6,2},{7,5},{8,12},{9,11},{10,... | collective-permute-start | bytes 786440 | tf_op jit(solution)/shard_map/send_f0/ppermute | solution.py:400
  17.8 85.0 %collective-permute-start.9 = (bf16[1,2,2,128,256]{4,3,2,1,0:T(8,128)(2,1)S(1)}, bf16[1,2,2,128,256]{4,3,2,1,0:T(8,128)(2,1)S(1)}, u32[]{:S(2)}, u32[]{:S(2)}) collective-permute-start(bf16[1,2,2,128,256]{4,3,2,1,0:T(8,128)(2,1)S(1)} %get-tuple-element.63), channel_id=1, source_target_pairs={{0,4},{1,3},{2,6},{3,1},{4,0},{5,7},{6,2},{7,5},{8,12},{9,11},{10,... | collective-permute-start | bytes 786440 | tf_op jit(solution)/shard_map/send_f1/ppermute | solution.py:400
  102.6 38.0 %collective-permute-start.8 = (bf16[256,1024]{1,0:T(8,128)(2,1)S(1)}, bf16[256,1024]{1,0:T(8,128)(2,1)S(1)}, u32[]{:S(2)}, u32[]{:S(2)}) collective-permute-start(bf16[256,1024]{1,0:T(8,128)(2,1)S(1)} %get-tuple-element.56), channel_id=1, source_target_pairs={{0,1},{1,0},{2,3},{3,2},{4,5},{5,4},{6,7},{7,6},{8,9},{9,8},{10,11... | collective-permute-start | bytes 1572872 | tf_op jit(solution)/shard_map/swap_out0/ppermute | solution.py:396
  130.2 47.7 %collective-permute-start.10 = (bf16[256,1024]{1,0:T(8,128)(2,1)S(1)}, bf16[256,1024]{1,0:T(8,128)(2,1)S(1)}, u32[]{:S(2)}, u32[]{:S(2)}) collective-permute-start(bf16[256,1024]{1,0:T(8,128)(2,1)S(1)} %stage.13), channel_id=1, source_target_pairs={{0,1},{1,0},{2,3},{3,2},{4,5},{5,4},{6,7},{7,6},{8,9},{9,8},{10,11... | collective-permute-start | bytes 1572872 | tf_op jit(solution)/shard_map/swap_out1/ppermute | solution.py:396
